TPU v7x, 32 devices: a whole 2x2x4 slice. The times are simulated.
32 devices in a mesh: grp: 4 (over y, core), tile: 8 (over z, x).
Axes of the slice: x: 2, y: 2, z: 4, core: 2. Of those that a mesh axis runs over, the one named last changes fastest.
Arguments:
- adjoint_state: float32 [64, 128, 2048], P('tile', 'grp'), may hold values from -6 to 6
- misfit: float32 [64, 128, 2048], P('tile', 'grp'), may hold values from -4 to 4
- east_speed: float32 [64, 128, 2048], P('tile', 'grp'), may hold values from -0.6 to 0.6
- north_speed: float32 [64, 128, 2048], P('tile', 'grp'), may hold values from -0.6 to 0.6
- land_mask: int32 [64, 128, 2048], P('tile', 'grp'), may hold values 0 or 1
- warming_forcing_selector: int32 [128, 2048], P('grp', 'tile'), may hold values 0 or 1
- vertical_filter_matrix: float32 [64, 64], replicated, may hold values from 0 to 0.54
Outputs:
- filtered_thermal_sensitivity: float32 [64, 128, 2048], P('tile', 'grp')
- boundary_warming_sensitivity: float32 [128, 2048], P('grp', 'tile')
All inputs are finite; a program needn't handle non-finite values. No bound on the sum of `land_mask` or of `warming_forcing_selector` on one device may be relied on, other than what follows from the above.
Results may differ from a plain program's by a relative error of at most 0.000088.
Values sent between devices are 32-bit elements; how exact they have to be, the bound alone decides.
A program may use at most 192 MiB of HBM per device.

v0:
```python
import jax
import jax.numpy as jnp
from jax import lax
from jax.sharding import PartitionSpec as P

STEPS = 2


def with_halo(cells, sides, width):
    for axis, dim in sides:
        count = lax.axis_size(axis)
        ends = count - 1
        head = lax.slice_in_dim(cells, 0, width, axis=dim)
        tail = lax.slice_in_dim(cells, cells.shape[dim] - width, cells.shape[dim], axis=dim)
        cells = jnp.concatenate(
            [
                lax.ppermute(tail, axis, [(i, (i + 1) % count) for i in range(ends)]),
                cells,
                lax.ppermute(head, axis, [((i + 1) % count, i) for i in range(ends)]),
            ],
            axis=dim,
        )
    return cells


def advance(padded, misfit, east_speed, north_speed, wet_cells):
    center = padded[1:-1, 1:-1, 1:-1]
    east_cell = padded[1:-1, 1:-1, 2:]
    western_neighbour = padded[1:-1, 1:-1, :-2]
    north_cell = padded[1:-1, 2:, 1:-1]
    south_cell = padded[1:-1, :-2, 1:-1]
    upper_cell = padded[:-2, 1:-1, 1:-1]
    lower_cell = padded[2:, 1:-1, 1:-1]
    vertical = upper_cell + lower_cell - 2.0 * center
    lateral = east_cell + western_neighbour + north_cell + south_cell - 4.0 * center
    change = 0.5 * east_speed * (east_cell - western_neighbour) + 0.5 * north_speed * (
        north_cell - south_cell
    )
    return wet_cells * (center + misfit + change + 0.1 * lateral + 0.15 * vertical)


def smooth_levels(vertical_filter_matrix, pencil):
    return jnp.einsum(
        "cz,zne->cne", vertical_filter_matrix, pencil, precision=lax.Precision.HIGHEST
    )


def body(
    adjoint_state,
    misfit,
    east_speed,
    north_speed,
    land_mask,
    warming_forcing_selector,
    vertical_filter_matrix,
):
    wet_cells = land_mask.astype(jnp.float32)
    current_tracer_values = adjoint_state
    for step_index in range(STEPS):
        bordered = with_halo(current_tracer_values, (("grp", 1), ("tile", 0)), 1)
        padded = jnp.pad(bordered, ((0, 0), (0, 0), (1, 1)))
        current_tracer_values = advance(padded, misfit, east_speed, north_speed, wet_cells)
    pencil = lax.all_to_all(current_tracer_values, "tile", split_axis=2, concat_axis=0, tiled=True)
    smoothed_field = smooth_levels(vertical_filter_matrix, pencil)
    surface_layer = smoothed_field[0]
    filtered_thermal_sensitivity = lax.all_to_all(
        smoothed_field, "tile", split_axis=0, concat_axis=2, tiled=True
    )
    boundary_warming_sensitivity = warming_forcing_selector.astype(jnp.float32) * surface_layer
    return (filtered_thermal_sensitivity, boundary_warming_sensitivity)


def solution(mesh):
    in_specs = (
        P("tile", "grp", None),
        P("tile", "grp", None),
        P("tile", "grp", None),
        P("tile", "grp", None),
        P("tile", "grp", None),
        P("grp", "tile"),
        P(),
    )
    out_specs = (P("tile", "grp", None), P("grp", "tile"))
    return jax.shard_map(body, mesh=mesh, in_specs=in_specs, out_specs=out_specs, check_vma=False)
```

profile of v0, /device:TPU:0, one launch (start us, length us, event | category | flops | bytes accessed | tf_op | source)
XLA Modules:
  0.0 217.6 jit_solution(6359021577452492257)
XLA Ops:
  0.7 1.4 fusion.18
  2.1 2.4 %collective-permute-start = (f32[8,1,2048]{2,0,1:T(8,128)S(1)}, f32[8,1,2048]{2,0,1:T(8,128)S(1)}, u32[]{:S(2)}, u32[]{:S(2)}) collective-permute-start(f32[8,1,2048]{2,0,1:T(8,128)S(1)} %copy.101), channel_id=1, source_target_pairs={{0,8},{8,16},{16,24},{1,9},{9,17},{17,25},{2,10},{10,18},{18,26},{... | collective-permute-start | bytes 196616 | tf_op jit(solution)/shard_map/ppermute | solution.py:17
  4.5 1.3 collective-permute-start.1
  5.9 3.9 %collective-permute-done.1 = f32[8,1,2048]{2,0,1:T(8,128)S(1)} collective-permute-done((f32[8,1,2048]{2,0,1:T(8,128)S(1)}, f32[8,1,2048]{2,0,1:T(8,128)S(1)}, u32[]{:S(2)}, u32[]{:S(2)}) %collective-permute-start.1) | collective-permute-done | bytes 65568 | tf_op jit(solution)/shard_map/ppermute | solution.py:19
  9.9 1.1 pad_maximum_fusion.21
  11.0 3.4 %collective-permute-start.2 = (f32[1,34,2048]{2,1,0:T(8,128)S(1)}, f32[1,34,2048]{2,1,0:T(8,128)S(1)}, u32[]{:S(2)}, u32[]{:S(2)}) collective-permute-start(f32[1,34,2048]{2,1,0:T(8,128)S(1)} %get-tuple-element.4), channel_id=1, source_target_pairs={{0,1},{1,2},{2,3},{3,4},{4,5},{5,6},{6,7},{8,9},{9,10},{10,11},{11... | collective-permute-start | bytes 835592 | tf_op jit(solution)/shard_map/ppermute | solution.py:17
  14.5 1.6 collective-permute-start.3
  16.0 4.3 %collective-permute-done.2 = f32[1,34,2048]{2,1,0:T(8,128)S(1)} collective-permute-done((f32[1,34,2048]{2,1,0:T(8,128)S(1)}, f32[1,34,2048]{2,1,0:T(8,128)S(1)}, u32[]{:S(2)}, u32[]{:S(2)}) %collective-permute-start.2) | collective-permute-done | bytes 278560 | tf_op jit(solution)/shard_map/ppermute | solution.py:17
  20.3 5.0 %collective-permute-done.3 = f32[1,34,2048]{2,1,0:T(8,128)S(1)} collective-permute-done((f32[1,34,2048]{2,1,0:T(8,128)S(1)}, f32[1,34,2048]{2,1,0:T(8,128)S(1)}, u32[]{:S(2)}, u32[]{:S(2)}) %collective-permute-start.3) | collective-permute-done | bytes 278560 | tf_op jit(solution)/shard_map/ppermute | solution.py:19
  25.3 3.1 %select_maximum_fusion.4 = f32[10,34,2050]{2,1,0:T(8,128)S(1)} fusion(f32[1,34,2048]{2,1,0:T(8,128)S(1)} %collective-permute-done.3, f32[1,34,2048]{2,1,0:T(8,128)S(1)} %collective-permute-done.2, f32[8,1,2048]{2,1,0:T(1,128)S(1)} %copy.87, f32[8,32,2048]{2,1,0:T(8,128)S(1)} %copy-done.1, f32[8,1,2048]{2,1,0:T(1,128)S(1)} %copy.86), kind=kLoop, calls=%fused_computation.6 | loop fusion | flops 8364000 | bytes 5573280 | tf_op jit(solution)/shard_map/concatenate | solution.py:15
  28.5 4.3 %fusion.10 = f32[8,32,2048]{2,1,0:T(8,128)S(1)} fusion(f32[1,34,2048]{2,1,0:T(8,128)S(1)} %collective-permute-done.3, f32[8,1,2048]{2,1,0:T(1,128)S(1)} %copy.87, f32[8,32,2048]{2,1,0:T(8,128)S(1)} %copy-done.1, f32[8,1,2048]{2,1,0:T(1,128)S(1)} %copy.86, f32[1,34,2048]{2,1,0:T(8,128)S(1)} %collective-permute-done.2, ...), kind=kLoop, calls=%fused_computation.29 | loop fusion | flops 16252928 | bytes 17465344 | tf_op jit(solution)/shard_map/mul | solution.py:39
  32.9 6.2 %collective-permute-start.4 = (f32[8,1,2048]{2,0,1:T(8,128)S(1)}, f32[8,1,2048]{2,0,1:T(8,128)S(1)}, u32[]{:S(2)}, u32[]{:S(2)}) collective-permute-start(f32[8,1,2048]{2,0,1:T(8,128)S(1)} %copy.90), channel_id=1, source_target_pairs={{0,8},{8,16},{16,24},{1,9},{9,17},{17,25},{2,10},{10,18},{18,26},{... | collective-permute-start | bytes 196616 | tf_op jit(solution)/shard_map/ppermute | solution.py:17
  39.1 1.3 collective-permute-start.5
  40.5 1.8 collective-permute-done.5
  42.5 4.1 %collective-permute-start.6 = (f32[1,34,2048]{2,1,0:T(8,128)S(1)}, f32[1,34,2048]{2,1,0:T(8,128)S(1)}, u32[]{:S(2)}, u32[]{:S(2)}) collective-permute-start(f32[1,34,2048]{2,1,0:T(8,128)S(1)} %get-tuple-element.2), channel_id=1, source_target_pairs={{0,1},{1,2},{2,3},{3,4},{4,5},{5,6},{6,7},{8,9},{9,10},{10,11},{11... | collective-permute-start | bytes 835592 | tf_op jit(solution)/shard_map/ppermute | solution.py:17
  46.6 1.4 collective-permute-start.7
  48.0 5.1 %collective-permute-done.6 = f32[1,34,2048]{2,1,0:T(8,128)S(1)} collective-permute-done((f32[1,34,2048]{2,1,0:T(8,128)S(1)}, f32[1,34,2048]{2,1,0:T(8,128)S(1)}, u32[]{:S(2)}, u32[]{:S(2)}) %collective-permute-start.6) | collective-permute-done | bytes 278560 | tf_op jit(solution)/shard_map/ppermute | solution.py:17
  53.1 5.2 %collective-permute-done.7 = f32[1,34,2048]{2,1,0:T(8,128)S(1)} collective-permute-done((f32[1,34,2048]{2,1,0:T(8,128)S(1)}, f32[1,34,2048]{2,1,0:T(8,128)S(1)}, u32[]{:S(2)}, u32[]{:S(2)}) %collective-permute-start.7) | collective-permute-done | bytes 278560 | tf_op jit(solution)/shard_map/ppermute | solution.py:19
  58.3 3.1 %select_maximum_fusion = f32[10,34,2050]{2,1,0:T(8,128)S(1)} fusion(f32[1,34,2048]{2,1,0:T(8,128)S(1)} %collective-permute-done.7, f32[1,34,2048]{2,1,0:T(8,128)S(1)} %collective-permute-done.6, f32[8,1,2048]{2,1,0:T(1,128)S(1)} %copy.93, f32[8,32,2048]{2,1,0:T(8,128)S(1)} %fusion.10, f32[8,1,2048]{2,1,0:T(1,128)S(1)} %copy.92), kind=kLoop, calls=%fused_computation.2 | loop fusion | flops 8364000 | bytes 5573280 | tf_op jit(solution)/shard_map/concatenate | solution.py:15
  61.4 3.0 %fusion.5 = f32[8,32,2048]{2,1,0:T(8,128)S(1)} fusion(f32[1,34,2048]{2,1,0:T(8,128)S(1)} %collective-permute-done.7, f32[8,1,2048]{2,1,0:T(1,128)S(1)} %copy.93, f32[8,32,2048]{2,1,0:T(8,128)S(1)} %fusion.10, f32[8,1,2048]{2,1,0:T(1,128)S(1)} %copy.92, f32[1,34,2048]{2,1,0:T(8,128)S(1)} %collective-permute-done.6, ...), kind=kLoop, calls=%fused_computation.16 | loop fusion | flops 16252928 | bytes 17465344 | tf_op jit(solution)/shard_map/mul | solution.py:39
  64.5 4.7 %copy.96 = f32[8,32,2048]{1,0,2:T(8,128)} copy(f32[8,32,2048]{2,1,0:T(8,128)S(1)} %fusion.5) | data formatting | bytes 4194304 | tf_op jit(solution)/shard_map/mul | solution.py:39
  69.2 7.4 %reshape.5 = f32[8,1,65536]{2,1,0:T(1,128)S(1)} reshape(f32[2048,8,32]{2,1,0:T(8,128)} %bitcast.22) | data formatting | bytes 4194304
  76.6 59.5 %all_to_all.36 = f32[8,1,65536]{2,1,0:T(1,128)} all-to-all(f32[8,1,65536]{2,1,0:T(1,128)S(1)} %reshape.5), channel_id=1, replica_groups=mesh['grp'=4,'tile'=8] {'tile'}, dimensions={0} | all-to-all | bytes 4194304 | tf_op jit(solution)/shard_map/all_to_all | solution.py:63
  136.7 7.2 %reduce = f32[8,65536]{1,0:T(8,128)S(1)} reduce(f32[8,1,65536]{2,1,0:T(1,128)} %all_to_all.36, f32[]{:T(128)} %broadcast.70), dimensions={1}, to_apply=%all_to_all.26.reduce_sub_computation | reduce | bytes 4194308 | tf_op jit(solution)/shard_map/all_to_all | solution.py:63
  143.9 6.0 %reshape.6 = f32[2048,8,32]{2,1,0:T(8,128)} reshape(f32[8,65536]{1,0:T(8,128)S(1)} %reduce) | data formatting | bytes 4194304
  149.9 6.6 %copy.97 = f32[8,32,8,256]{3,0,2,1:T(8,128)} copy(f32[8,32,8,256]{1,0,3,2:T(8,128)} %bitcast.23) | data formatting | bytes 4194304 | tf_op jit(solution)/shard_map/all_to_all | solution.py:63
  156.5 3.6 %fusion.13 = f32[64,32,256]{2,0,1:T(8,128)S(1)} fusion(f32[8,32,8,256]{3,0,2,1:T(8,128)} %copy.97, f32[64,64]{1,0:T(8,128)S(1)} %copy-done), kind=kOutput, calls=%fused_computation.39 | convolution fusion | flops 402653184 | bytes 4210688 | tf_op jit(solution)/shard_map/cz,zne->cne/dot_general | solution.py:43
  160.1 2.5 %copy.98 = f32[64,32,256]{2,1,0:T(8,128)} copy(f32[64,32,256]{2,0,1:T(8,128)S(1)} %fusion.13) | data formatting | bytes 4194304 | tf_op jit(solution)/shard_map/cz,zne->cne/dot_general | solution.py:43
  162.6 4.5 %all-to-all-start.1 = ((f32[64,32,256]{2,1,0:T(8,128)}), f32[64,32,256]{2,1,0:T(8,128)}, u32[]{:S(2)}, u32[]{:S(2)}) async-start(f32[64,32,256]{2,1,0:T(8,128)} %copy.98), calls=%async_computation.1 | async-start | bytes 4194304 | tf_op jit(solution)/shard_map/all_to_all | solution.py:66
  167.1 0.6 bitcast_multiply_fusion
  167.8 46.7 %all-to-all-done.1 = f32[64,32,256]{2,1,0:T(8,128)} async-done(((f32[64,32,256]{2,1,0:T(8,128)}), f32[64,32,256]{2,1,0:T(8,128)}, u32[]{:S(2)}, u32[]{:S(2)}) %all-to-all-start.1) | async-done | bytes 2097184 | tf_op jit(solution)/shard_map/all_to_all | solution.py:66
  214.4 3.2 %copy.103 = f32[8,8,4,8,256]{4,3,0,2,1:T(8,128)} copy(f32[8,8,4,8,256]{4,3,2,1,0:T(8,128)} %bitcast.10) | data formatting | bytes 4194304 | tf_op jit(solution)/shard_map/all_to_all | solution.py:66
  (28 shorter events, 1.1 us)
Async XLA Ops:
  0.6 155.8 %copy-start = (f32[64,64]{1,0:T(8,128)S(1)}, f32[64,64]{1,0:T(8,128)}, u32[]{:S(2)}) copy-start(f32[64,64]{1,0:T(8,128)} %param.13) | copy-start | bytes 49156
  0.6 24.7 %copy-start.1 = (f32[8,32,2048]{2,1,0:T(8,128)S(1)}, f32[8,32,2048]{2,1,0:T(8,128)}, u32[]{:S(2)}) copy-start(f32[8,32,2048]{2,1,0:T(8,128)} %param.7) | copy-start | bytes 6291460
  2.1 3.7 %collective-permute-start = (f32[8,1,2048]{2,0,1:T(8,128)S(1)}, f32[8,1,2048]{2,0,1:T(8,128)S(1)}, u32[]{:S(2)}, u32[]{:S(2)}) collective-permute-start(f32[8,1,2048]{2,0,1:T(8,128)S(1)} %copy.101), channel_id=1, source_target_pairs={{0,8},{8,16},{16,24},{1,9},{9,17},{17,25},{2,10},{10,18},{18,26},{... | collective-permute-start | bytes 196616 | tf_op jit(solution)/shard_map/ppermute | solution.py:17
  4.5 5.3 %collective-permute-start.1 = (f32[8,1,2048]{2,0,1:T(8,128)S(1)}, f32[8,1,2048]{2,0,1:T(8,128)S(1)}, u32[]{:S(2)}, u32[]{:S(2)}) collective-permute-start(f32[8,1,2048]{2,0,1:T(8,128)S(1)} %copy.102), channel_id=1, source_target_pairs={{8,0},{16,8},{24,16},{9,1},{17,9},{25,17},{10,2},{18,10},{26,18},{... | collective-permute-start | bytes 196616 | tf_op jit(solution)/shard_map/ppermute | solution.py:19
  11.0 9.3 %collective-permute-start.2 = (f32[1,34,2048]{2,1,0:T(8,128)S(1)}, f32[1,34,2048]{2,1,0:T(8,128)S(1)}, u32[]{:S(2)}, u32[]{:S(2)}) collective-permute-start(f32[1,34,2048]{2,1,0:T(8,128)S(1)} %get-tuple-element.4), channel_id=1, source_target_pairs={{0,1},{1,2},{2,3},{3,4},{4,5},{5,6},{6,7},{8,9},{9,10},{10,11},{11... | collective-permute-start | bytes 835592 | tf_op jit(solution)/shard_map/ppermute | solution.py:17
  14.4 14.0 %copy-start.2 = (f32[8,32,2048]{2,1,0:T(8,128)S(1)}, f32[8,32,2048]{2,1,0:T(8,128)}, u32[]{:S(2)}) copy-start(f32[8,32,2048]{2,1,0:T(8,128)} %param.8) | copy-start | bytes 6291460
  14.4 14.0 %copy-start.3 = (s32[8,32,2048]{2,1,0:T(8,128)S(1)}, s32[8,32,2048]{2,1,0:T(8,128)}, u32[]{:S(2)}) copy-start(s32[8,32,2048]{2,1,0:T(8,128)} %param.11) | copy-start | bytes 6291460
  14.5 14.0 %copy-start.4 = (f32[8,32,2048]{2,1,0:T(8,128)S(1)}, f32[8,32,2048]{2,1,0:T(8,128)}, u32[]{:S(2)}) copy-start(f32[8,32,2048]{2,1,0:T(8,128)} %param.10) | copy-start | bytes 6291460
  14.5 10.9 %collective-permute-start.3 = (f32[1,34,2048]{2,1,0:T(8,128)S(1)}, f32[1,34,2048]{2,1,0:T(8,128)S(1)}, u32[]{:S(2)}, u32[]{:S(2)}) collective-permute-start(f32[1,34,2048]{2,1,0:T(8,128)S(1)} %get-tuple-element.5), channel_id=1, source_target_pairs={{1,0},{2,1},{3,2},{4,3},{5,4},{6,5},{7,6},{9,8},{10,9},{11,10},{12... | collective-permute-start | bytes 835592 | tf_op jit(solution)/shard_map/ppermute | solution.py:19
  32.9 7.6 %collective-permute-start.4 = (f32[8,1,2048]{2,0,1:T(8,128)S(1)}, f32[8,1,2048]{2,0,1:T(8,128)S(1)}, u32[]{:S(2)}, u32[]{:S(2)}) collective-permute-start(f32[8,1,2048]{2,0,1:T(8,128)S(1)} %copy.90), channel_id=1, source_target_pairs={{0,8},{8,16},{16,24},{1,9},{9,17},{17,25},{2,10},{10,18},{18,26},{... | collective-permute-start | bytes 196616 | tf_op jit(solution)/shard_map/ppermute | solution.py:17
  39.1 3.1 %collective-permute-start.5 = (f32[8,1,2048]{2,0,1:T(8,128)S(1)}, f32[8,1,2048]{2,0,1:T(8,128)S(1)}, u32[]{:S(2)}, u32[]{:S(2)}) collective-permute-start(f32[8,1,2048]{2,0,1:T(8,128)S(1)} %copy.91), channel_id=1, source_target_pairs={{8,0},{16,8},{24,16},{9,1},{17,9},{25,17},{10,2},{18,10},{26,18},{... | collective-permute-start | bytes 196616 | tf_op jit(solution)/shard_map/ppermute | solution.py:19
  42.5 10.6 %collective-permute-start.6 = (f32[1,34,2048]{2,1,0:T(8,128)S(1)}, f32[1,34,2048]{2,1,0:T(8,128)S(1)}, u32[]{:S(2)}, u32[]{:S(2)}) collective-permute-start(f32[1,34,2048]{2,1,0:T(8,128)S(1)} %get-tuple-element.2), channel_id=1, source_target_pairs={{0,1},{1,2},{2,3},{3,4},{4,5},{5,6},{6,7},{8,9},{9,10},{10,11},{11... | collective-permute-start | bytes 835592 | tf_op jit(solution)/shard_map/ppermute | solution.py:17
  46.6 14.8 %copy-start.5 = (f32[8,32,2048]{2,1,0:T(8,128)S(1)}, f32[8,32,2048]{2,1,0:T(8,128)}, u32[]{:S(2)}) copy-start(f32[8,32,2048]{2,1,0:T(8,128)} %param.9) | copy-start | bytes 6291460
  46.6 11.7 %collective-permute-start.7 = (f32[1,34,2048]{2,1,0:T(8,128)S(1)}, f32[1,34,2048]{2,1,0:T(8,128)S(1)}, u32[]{:S(2)}, u32[]{:S(2)}) collective-permute-start(f32[1,34,2048]{2,1,0:T(8,128)S(1)} %get-tuple-element.3), channel_id=1, source_target_pairs={{1,0},{2,1},{3,2},{4,3},{5,4},{6,5},{7,6},{9,8},{10,9},{11,10},{12... | collective-permute-start | bytes 835592 | tf_op jit(solution)/shard_map/ppermute | solution.py:19
  162.6 4.5 %copy-start.6 = (s32[32,256]{1,0:T(8,128)S(1)}, s32[32,256]{1,0:T(8,128)}, u32[]{:S(2)}) copy-start(s32[32,256]{1,0:T(8,128)} %param.12) | copy-start | bytes 98308
  162.6 51.8 %all-to-all-start.1 = ((f32[64,32,256]{2,1,0:T(8,128)}), f32[64,32,256]{2,1,0:T(8,128)}, u32[]{:S(2)}, u32[]{:S(2)}) async-start(f32[64,32,256]{2,1,0:T(8,128)} %copy.98), calls=%async_computation.1 | async-start | bytes 4194304 | tf_op jit(solution)/shard_map/all_to_all | solution.py:66
where the time goes:
time: 218 us
  waiting for transfers between devices  71.9 us (33%)
  blocking collectives  59.5 us (27%)
  local copies, waits for them, and re-layouts  32.9 us (15%)
  starting transfers between devices  26.2 us (12%)
  other arithmetic  22.6 us (10%)
  matrix products  3.6 us (2%)
    all_to_all x1, blocking collectives, body(): lax.all_to_all(current_tracer_values, 'tile', split_axis=2, concat_axis=0...  59.5 us
    all_to_all x1, waiting for transfers between devices, body(): lax.all_to_all(smoothed_field, 'tile', split_axis=0, concat_axis=2, tiled...  46.7 us
    ppermute x4, starting transfers between devices, with_halo(): lax.ppermute(tail, axis, [(i, (i + 1) % count) for i in range(ends)])  16.1 us
    ppermute x4, waiting for transfers between devices, with_halo(): lax.ppermute(head, axis, [((i + 1) % count, i) for i in range(ends)])  15.8 us
    unnamed x18, local copies, waits for them, and re-layouts  13.5 us
    ppermute x4, waiting for transfers between devices, with_halo(): lax.ppermute(tail, axis, [(i, (i + 1) % count) for i in range(ends)])  9.4 us
    mul x2, other arithmetic, advance(): wet_cells * (center + misfit + change + 0.1 * lateral + 0.15 * vertical)  7.31 us
    all_to_all x1, other arithmetic, body(): lax.all_to_all(current_tracer_values, 'tile', split_axis=2, concat_axis=0...  7.22 us
  transfers between devices with their start and end apart: 9, of which 7 were waited for; matrix products, arithmetic and copies ran while one was open for 0% of the time, Pallas kernels for 0%

commit v1 on v0

v1 whole, which is shorter than its diff:
```python
import functools

import jax
import jax.numpy as jnp
from jax import lax
from jax.experimental import pallas as pl
from jax.experimental.pallas import tpu as pltpu
from jax.sharding import PartitionSpec as P

MESH = pl.DeviceIdType.MESH
SUB = 8
LANE = 128
WIDTH = 512
HIGHEST = lax.Precision.HIGHEST


def kernel(
    tiles,
    grps,
    state_ref,
    misfit_ref,
    east_ref,
    north_ref,
    land_ref,
    select_ref,
    matrix_ref,
    out_ref,
    surface_ref,
    s0,
    s1,
    s2,
    misfit,
    east,
    north,
    land,
    pencil,
    smooth,
    kron,
    load_sem,
    level_send,
    level_recv,
    row_send,
    row_recv,
    fwd_send,
    fwd_recv,
    ret_send,
    ret_recv,
):
    levels, rows, columns = state_ref.shape
    chunks = rows // SUB
    part = columns // tiles
    near = min(2, levels // 2)
    tile = lax.axis_index("tile")
    grp = lax.axis_index("grp")
    inner = (pl.ds(SUB, rows), pl.ds(LANE, columns))

    loads = [
        pltpu.make_async_copy(state_ref, s0.at[(pl.ds(1, levels),) + inner], load_sem.at[0]),
        pltpu.make_async_copy(misfit_ref, misfit, load_sem.at[1]),
        pltpu.make_async_copy(east_ref, east, load_sem.at[2]),
        pltpu.make_async_copy(north_ref, north, load_sem.at[3]),
        pltpu.make_async_copy(land_ref, land, load_sem.at[4]),
    ]
    for load in loads:
        load.start()

    barrier = pltpu.get_barrier_semaphore()

    @pl.loop(1, tiles)
    def _(i):
        other = lax.rem(tile + i, tiles)
        pl.semaphore_signal(barrier, inc=1, device_id=(grp, other), device_id_type=MESH)

    @pl.when(grp > 0)
    def _():
        pl.semaphore_signal(barrier, inc=1, device_id=(grp - 1, tile), device_id_type=MESH)

    @pl.when(grp < grps - 1)
    def _():
        pl.semaphore_signal(barrier, inc=1, device_id=(grp + 1, tile), device_id_type=MESH)

    for buf in (s0, s1):
        for start in (0, columns + LANE):
            buf[1 : levels + 1, SUB : SUB + rows, start : start + LANE] = jnp.zeros(
                (levels, rows, LANE), jnp.float32
            )

        @pl.when(tile == 0)
        def _():
            buf[0, SUB : SUB + rows, :] = jnp.zeros((rows, columns + 2 * LANE), jnp.float32)

        @pl.when(tile == tiles - 1)
        def _():
            buf[levels + 1, SUB : SUB + rows, :] = jnp.zeros((rows, columns + 2 * LANE), jnp.float32)

        @pl.when(grp == 0)
        def _():
            buf[1 : levels + 1, 0:SUB, :] = jnp.zeros((levels, SUB, columns + 2 * LANE), jnp.float32)

        @pl.when(grp == grps - 1)
        def _():
            buf[1 : levels + 1, SUB + rows :, :] = jnp.zeros(
                (levels, SUB, columns + 2 * LANE), jnp.float32
            )

    beside = (grp > 0).astype(jnp.int32) + (grp < grps - 1).astype(jnp.int32)
    pl.semaphore_wait(barrier, tiles - 1 + beside)

    def level_copies(buf, step):
        top, bottom = state_ref.at[0], state_ref.at[levels - 1]
        if step:
            top, bottom = buf.at[(1,) + inner], buf.at[(levels,) + inner]
        return [
            (
                tile > 0,
                tile < tiles - 1,
                pltpu.make_async_remote_copy(
                    top,
                    buf.at[(levels + 1,) + inner],
                    level_send.at[step, 0],
                    level_recv.at[step, 0],
                    (grp, tile - 1),
                    MESH,
                ),
            ),
            (
                tile < tiles - 1,
                tile > 0,
                pltpu.make_async_remote_copy(
                    bottom,
                    buf.at[(0,) + inner],
                    level_send.at[step, 1],
                    level_recv.at[step, 1],
                    (grp, tile + 1),
                    MESH,
                ),
            ),
        ]

    def row_copies(buf, step, slot, first, count):
        span = pl.ds(first + 1, count)
        across = pl.ds(LANE, columns)
        top, bottom = state_ref.at[:, pl.ds(0, 1), :], state_ref.at[:, pl.ds(rows - 1, 1), :]
        if step:
            top = buf.at[span, pl.ds(SUB, 1), across]
            bottom = buf.at[span, pl.ds(SUB + rows - 1, 1), across]
        return [
            (
                grp > 0,
                grp < grps - 1,
                pltpu.make_async_remote_copy(
                    top,
                    buf.at[span, pl.ds(SUB + rows, 1), across],
                    row_send.at[slot, 0],
                    row_recv.at[slot, 0],
                    (grp - 1, tile),
                    MESH,
                ),
            ),
            (
                grp < grps - 1,
                grp > 0,
                pltpu.make_async_remote_copy(
                    bottom,
                    buf.at[span, pl.ds(SUB - 1, 1), across],
                    row_send.at[slot, 1],
                    row_recv.at[slot, 1],
                    (grp + 1, tile),
                    MESH,
                ),
            ),
        ]

    def start(copies):
        for sends, _, copy in copies:
            pl.when(sends)(copy.start)

    def arrive(copies):
        for _, receives, copy in copies:
            pl.when(receives)(copy.wait_recv)

    def leave(copies):
        for sends, _, copy in copies:
            pl.when(sends)(copy.wait_send)

    sub_index = lax.broadcasted_iota(jnp.int32, (SUB, WIDTH), 0)

    def advance(src, dst, pad, first, count, row_first, row_count):
        if count <= 0:
            return

        @pl.loop(0, count * row_count)
        def _(i):
            level = first + lax.div(i, row_count)
            row = pl.multiple_of((row_first + lax.rem(i, row_count)) * SUB, SUB)
            for at in range(0, columns, WIDTH):
                here = pl.ds(at, WIDTH)
                mid = pl.ds(at + LANE, WIDTH)
                wide = src[level + 1, pl.ds(row + SUB, SUB), pl.ds(at, WIDTH + 2 * LANE)]
                center = wide[:, LANE : LANE + WIDTH]
                e = pltpu.roll(wide, WIDTH + 2 * LANE - 1, 1)[:, LANE : LANE + WIDTH]
                w = pltpu.roll(wide, 1, 1)[:, LANE : LANE + WIDTH]
                up = src[level + 1, pl.ds(row, SUB), mid]
                down = src[level + 1, pl.ds(row + 2 * SUB, SUB), mid]
                n = pltpu.roll(jnp.where(sub_index == 0, down, center), SUB - 1, 0)
                s = pltpu.roll(jnp.where(sub_index == SUB - 1, up, center), 1, 0)
                a = src[level, pl.ds(row + SUB, SUB), mid]
                b = src[level + 2, pl.ds(row + SUB, SUB), mid]
                rr = pl.ds(row, SUB)
                flow = east[level, rr, here] * (e - w) + north[level, rr, here] * (n - s)
                value = (
                    (0.3 * center + misfit[level, rr, here])
                    + 0.5 * flow
                    + (0.1 * ((e + w) + (n + s)) + 0.15 * (a + b))
                )
                value = land[level, rr, here].astype(jnp.float32) * value
                if pad:
                    dst[level + 1, pl.ds(row + SUB, SUB), mid] = value
                else:
                    dst[level, rr, here] = value

    def forward(first, count, row_first, row_count):
        if count <= 0:
            return
        for r in range(row_first, row_first + row_count):
            span = pl.ds(r * SUB, SUB)
            target = pencil.at[pl.ds(tile * levels + first, count), span, :]

            @pl.loop(1, tiles)
            def _(i):
                other = lax.rem(tile + i, tiles)
                mine = pl.ds(pl.multiple_of(other * part, LANE), part)
                pltpu.make_async_remote_copy(
                    s2.at[pl.ds(first, count), span, mine],
                    target,
                    fwd_send,
                    fwd_recv.at[r],
                    (grp, other),
                    MESH,
                ).start()

            own = pl.ds(pl.multiple_of(tile * part, LANE), part)
            pltpu.make_async_copy(
                s2.at[pl.ds(first, count), span, own], target, fwd_recv.at[r]
            ).start()

    level0 = level_copies(s0, 0)
    row0 = row_copies(s0, 0, 0, 0, levels)
    start(row0)
    start(level0)
    for load in loads:
        load.wait()
    arrive(row0)

    advance(s0, s1, True, 1, levels - 2, 0, chunks)
    level1 = level_copies(s1, 1)
    row_mid = row_copies(s1, 1, 1, 1, levels - 2) if levels > 2 else []
    row_ends = row_copies(s1, 1, 2, 0, 1) + row_copies(s1, 1, 3, levels - 1, 1)
    start(row_mid)

    early = levels - 2 * near
    advance(s1, s2, False, near, early, 1, chunks - 2)
    forward(near, early, 1, chunks - 2)

    arrive(level0)
    advance(s0, s1, True, 0, 1, 0, chunks)
    advance(s0, s1, True, levels - 1, 1, 0, chunks)
    start(level1)
    start(row_ends)

    arrive(row_mid)
    for r in (0, chunks - 1):
        advance(s1, s2, False, near, early, r, 1)
        forward(near, early, r, 1)
    advance(s1, s2, False, 1, near - 1, 0, chunks)
    advance(s1, s2, False, levels - near, near - 1, 0, chunks)

    size = tiles * levels * SUB
    repeat = (
        lax.shift_right_logical(lax.broadcasted_iota(jnp.int32, (size, tiles * levels), 0), 3)
        == lax.broadcasted_iota(jnp.int32, (size, tiles * levels), 1)
    ).astype(jnp.float32)
    tall = jnp.dot(repeat, matrix_ref[...], precision=HIGHEST, preferred_element_type=jnp.float32)
    full = lax.dot_general(
        tall,
        repeat,
        (((1,), (1,)), ((), ())),
        precision=HIGHEST,
        preferred_element_type=jnp.float32,
    )
    same = (lax.broadcasted_iota(jnp.int32, (size, size), 0) & (SUB - 1)) == (
        lax.broadcasted_iota(jnp.int32, (size, size), 1) & (SUB - 1)
    )
    kron[...] = jnp.where(same, full, 0.0)

    arrive(level1)
    arrive(row_ends)
    order = list(range(1, chunks - 1)) + [0, chunks - 1]
    for r in order:
        advance(s1, s2, False, 0, 1, r, 1)
        advance(s1, s2, False, levels - 1, 1, r, 1)
        forward(0, near, r, 1)
        forward(levels - near, near, r, 1)

    for r in order:
        span = pl.ds(r * SUB, SUB)
        chunk = pencil.at[:, span, :]
        pltpu.make_async_copy(chunk, chunk, fwd_recv.at[r]).wait()
        result = jnp.dot(
            kron[...],
            pencil[:, r * SUB : (r + 1) * SUB, :].reshape(size, part),
            precision=HIGHEST,
            preferred_element_type=jnp.float32,
        )
        smooth[:, r * SUB : (r + 1) * SUB, :] = result.reshape(tiles * levels, SUB, part)
        home = out_ref.at[:, span, pl.ds(pl.multiple_of(tile * part, LANE), part)]

        @pl.loop(1, tiles)
        def _(i):
            other = lax.rem(tile + i, tiles)
            pltpu.make_async_remote_copy(
                smooth.at[pl.ds(other * levels, levels), span, :],
                home,
                ret_send,
                ret_recv,
                (grp, other),
                MESH,
            ).start()

        pltpu.make_async_copy(
            smooth.at[pl.ds(tile * levels, levels), span, :], home, ret_recv
        ).start()
        surface_ref[r * SUB : (r + 1) * SUB, :] = (
            select_ref[r * SUB : (r + 1) * SUB, :].astype(jnp.float32) * result[0:SUB]
        )

    for copies in (level0, row0, level1, row_mid, row_ends):
        leave(copies)
    sent = s2.at[:, :, pl.ds(0, (tiles - 1) * part)]
    pltpu.make_async_copy(sent, sent, fwd_send).wait()
    returned = smooth.at[pl.ds(0, (tiles - 1) * levels)]
    pltpu.make_async_copy(returned, returned, ret_send).wait()
    pltpu.make_async_copy(out_ref, out_ref, ret_recv).wait()


def body(tiles, grps, *args):
    levels, rows, columns = args[0].shape
    part = columns // tiles
    total = tiles * levels
    padded = (levels + 2, rows + 2 * SUB, columns + 2 * LANE)
    block = (levels, rows, columns)
    anywhere = pl.BlockSpec(memory_space=pl.ANY)
    vmem = pl.BlockSpec(memory_space=pltpu.VMEM)
    return pl.pallas_call(
        functools.partial(kernel, tiles, grps),
        out_shape=(
            jax.ShapeDtypeStruct(block, jnp.float32),
            jax.ShapeDtypeStruct((rows, part), jnp.float32),
        ),
        in_specs=[anywhere] * 5 + [vmem] * 2,
        out_specs=(anywhere, vmem),
        scratch_shapes=[
            pltpu.VMEM(padded, jnp.float32),
            pltpu.VMEM(padded, jnp.float32),
            pltpu.VMEM(block, jnp.float32),
            pltpu.VMEM(block, jnp.float32),
            pltpu.VMEM(block, jnp.float32),
            pltpu.VMEM(block, jnp.float32),
            pltpu.VMEM(block, jnp.int32),
            pltpu.VMEM((total, rows, part), jnp.float32),
            pltpu.VMEM((total, rows, part), jnp.float32),
            pltpu.VMEM((total * SUB, total * SUB), jnp.float32),
            pltpu.SemaphoreType.DMA((5,)),
            pltpu.SemaphoreType.DMA((2, 2)),
            pltpu.SemaphoreType.DMA((2, 2)),
            pltpu.SemaphoreType.DMA((4, 2)),
            pltpu.SemaphoreType.DMA((4, 2)),
            pltpu.SemaphoreType.DMA,
            pltpu.SemaphoreType.DMA((rows // SUB,)),
            pltpu.SemaphoreType.DMA,
            pltpu.SemaphoreType.DMA,
        ],
        compiler_params=pltpu.CompilerParams(
            collective_id=0, has_side_effects=True, vmem_limit_bytes=56 * 1024 * 1024
        ),
    )(*args)


def solution(mesh):
    split = P("tile", "grp", None)
    return jax.shard_map(
        functools.partial(body, mesh.shape["tile"], mesh.shape["grp"]),
        mesh=mesh,
        in_specs=(split,) * 5 + (P("grp", "tile"), P()),
        out_specs=(split, P("grp", "tile")),
        check_vma=False,
    )
```

time: 218 us -> 114 us (0.52)
  Pallas kernels: 0 us -> 108 us
  waiting for transfers between devices: 71.9 us -> 0 us
  blocking collectives: 59.5 us -> 0 us
  local copies, waits for them, and re-layouts: 32.9 us -> 3.76 us
  starting transfers between devices: 26.2 us -> 0 us
  other arithmetic: 22.6 us -> 0 us
  matrix products: 3.6 us -> 0 us
    pallas_call x0 -> x1, Pallas kernels: none -> 108 us  [body(): pl.pallas_call(functools.partial(kernel, tiles, grps), out_shape=(jax.Sha...]
    all_to_all x1 -> x0, blocking collectives: 59.5 us -> none  [body(): lax.all_to_all(current_tracer_values, 'tile', split_axis=2, concat_axis=0...]
    all_to_all x1 -> x0, waiting for transfers between devices: 46.7 us -> none  [body(): lax.all_to_all(smoothed_field, 'tile', split_axis=0, concat_axis=2, tiled...]
    ppermute x8 -> x0, waiting for transfers between devices: 25.2 us -> none  [the longest x4 15.8 us: with_halo(): lax.ppermute(head, axis, [((i + 1) % count, i) for i in range(ends)])]
    ppermute x8 -> x0, starting transfers between devices: 21.7 us -> none  [the longest x4 16.1 us: with_halo(): lax.ppermute(tail, axis, [(i, (i + 1) % count) for i in range(ends)])]
    all_to_all x3 -> x0, local copies, waits for them, and re-layouts: 10.3 us -> none  [the longest x2 7.09 us: body(): lax.all_to_all(current_tracer_values, 'tile', split_axis=2, concat_axis=0...]
    unnamed x18 -> x4, local copies, waits for them, and re-layouts: 13.5 us -> 3.76 us
    mul x3 -> x0, other arithmetic: 7.93 us -> none  [the longest x2 7.31 us: advance(): wet_cells * (center + misfit + change + 0.1 * lateral + 0.15 * vertical)]
  transfers between devices with their start and end apart: 9 -> 0, of which waited for: 7 -> 0; matrix products, arithmetic and copies ran while one was open for 0% -> 0% of each run, Pallas kernels for 0% -> 0%
where the time goes in v1:
time: 114 us; the launch traced here: 113 us
  Pallas kernels  108 us (95%)
  local copies, waits for them, and re-layouts  3.76 us (3%)
    pallas_call x1, Pallas kernels, body(): pl.pallas_call(functools.partial(kernel, tiles, grps), out_shape=(jax.Sha...  108 us
    unnamed x4, local copies, waits for them, and re-layouts  3.76 us

profile of v1, /device:TPU:0, one launch (start us, length us, event | category | flops | bytes accessed | tf_op | source)
XLA Modules:
  0.0 112.7 jit_solution(13115642137768778958)
XLA Ops:
  0.6 108.3 %shard_map.86 = (f32[8,32,2048]{2,1,0:T(8,128)}, f32[32,256]{1,0:T(8,128)}) custom-call(f32[8,32,2048]{2,1,0:T(8,128)} %state_ref.1, f32[8,32,2048]{2,1,0:T(8,128)} %misfit_ref.1, f32[8,32,2048]{2,1,0:T(8,128)} %east_ref.1, f32[8,32,2048]{2,1,0:T(8,128)} %north_ref.1, s32[8,32,2048]{2,1,0:T(8,128)} %land_ref.1, s32[32,256]{1,0:T(8,128)} %select_ref.1, ...), custom_call_target="tpu_custom_call" | custom-call | tf_op jit(solution)/shard_map/pallas_call | solution.py:354
  109.0 0.0 copy-start
  109.0 3.1 %copy.11 = f32[8,32,2048]{2,1,0:T(8,128)} copy(f32[8,32,2048]{2,1,0:T(8,128)} %get-tuple-element.4) | data formatting | bytes 4194304
  112.1 0.0 copy-done
  112.1 0.6 copy.12
Async XLA Ops:
  109.0 3.2 %copy-start = (f32[32,256]{1,0:T(8,128)S(1)}, f32[32,256]{1,0:T(8,128)}, u32[]{:S(2)}) copy-start(f32[32,256]{1,0:T(8,128)} %get-tuple-element.5) | copy-start | bytes 98308

commit v2 on v1

--- a/solution.py
+++ b/solution.py
@@ -22,7 +22,6 @@
     east_ref,
     north_ref,
     land_ref,
-    select_ref,
     matrix_ref,
     out_ref,
     surface_ref,
@@ -250,23 +249,27 @@
     start(level0)
     for load in loads:
         load.wait()
-    arrive(row0)
-
-    advance(s0, s1, True, 1, levels - 2, 0, chunks)
+
     level1 = level_copies(s1, 1)
     row_mid = row_copies(s1, 1, 1, 1, levels - 2) if levels > 2 else []
     row_ends = row_copies(s1, 1, 2, 0, 1) + row_copies(s1, 1, 3, levels - 1, 1)
+    early = levels - 2 * near
+    middle = chunks - 2
+    advance(s0, s1, True, 1, levels - 2, 1, middle)
+    arrive(row0)
+    advance(s0, s1, True, 1, levels - 2, 0, 1)
+    for r in range(1, middle):
+        advance(s1, s2, False, near, early, r, 1)
+        forward(near, early, r, 1)
+    advance(s0, s1, True, 1, levels - 2, chunks - 1, 1)
     start(row_mid)
-
-    early = levels - 2 * near
-    advance(s1, s2, False, near, early, 1, chunks - 2)
-    forward(near, early, 1, chunks - 2)
-
     arrive(level0)
     advance(s0, s1, True, 0, 1, 0, chunks)
     advance(s0, s1, True, levels - 1, 1, 0, chunks)
     start(level1)
     start(row_ends)
+    advance(s1, s2, False, near, early, middle, 1)
+    forward(near, early, middle, 1)
 
     arrive(row_mid)
     for r in (0, chunks - 1):
@@ -274,6 +277,15 @@
         forward(near, early, r, 1)
     advance(s1, s2, False, 1, near - 1, 0, chunks)
     advance(s1, s2, False, levels - near, near - 1, 0, chunks)
+
+    arrive(level1)
+    arrive(row_ends)
+    order = list(range(1, chunks - 1)) + [0, chunks - 1]
+    for r in order:
+        advance(s1, s2, False, 0, 1, r, 1)
+        advance(s1, s2, False, levels - 1, 1, r, 1)
+        forward(0, near, r, 1)
+        forward(levels - near, near, r, 1)
 
     size = tiles * levels * SUB
     repeat = (
@@ -293,15 +305,6 @@
     )
     kron[...] = jnp.where(same, full, 0.0)
 
-    arrive(level1)
-    arrive(row_ends)
-    order = list(range(1, chunks - 1)) + [0, chunks - 1]
-    for r in order:
-        advance(s1, s2, False, 0, 1, r, 1)
-        advance(s1, s2, False, levels - 1, 1, r, 1)
-        forward(0, near, r, 1)
-        forward(levels - near, near, r, 1)
-
     for r in order:
         span = pl.ds(r * SUB, SUB)
         chunk = pencil.at[:, span, :]
@@ -330,9 +333,7 @@
         pltpu.make_async_copy(
             smooth.at[pl.ds(tile * levels, levels), span, :], home, ret_recv
         ).start()
-        surface_ref[r * SUB : (r + 1) * SUB, :] = (
-            select_ref[r * SUB : (r + 1) * SUB, :].astype(jnp.float32) * result[0:SUB]
-        )
+        surface_ref[r * SUB : (r + 1) * SUB, :] = result[0:SUB]
 
     for copies in (level0, row0, level1, row_mid, row_ends):
         leave(copies)
@@ -344,6 +345,7 @@
 
 
 def body(tiles, grps, *args):
+    args, select = args[:5] + args[6:], args[5]
     levels, rows, columns = args[0].shape
     part = columns // tiles
     total = tiles * levels
@@ -351,13 +353,13 @@
     block = (levels, rows, columns)
     anywhere = pl.BlockSpec(memory_space=pl.ANY)
     vmem = pl.BlockSpec(memory_space=pltpu.VMEM)
-    return pl.pallas_call(
+    filtered, surface = pl.pallas_call(
         functools.partial(kernel, tiles, grps),
         out_shape=(
             jax.ShapeDtypeStruct(block, jnp.float32),
             jax.ShapeDtypeStruct((rows, part), jnp.float32),
         ),
-        in_specs=[anywhere] * 5 + [vmem] * 2,
+        in_specs=[anywhere] * 5 + [vmem],
         out_specs=(anywhere, vmem),
         scratch_shapes=[
             pltpu.VMEM(padded, jnp.float32),
@@ -384,6 +386,7 @@
             collective_id=0, has_side_effects=True, vmem_limit_bytes=56 * 1024 * 1024
         ),
     )(*args)
+    return filtered, select.astype(jnp.float32) * surface
 
 
 def solution(mesh):

time: 114 us -> 120 us (1.053)
  Pallas kernels: 108 us -> 113 us
  other arithmetic: 0 us -> 1.38 us
    pallas_call x1, Pallas kernels: 108 us -> 113 us  [body(): pl.pallas_call(functools.partial(kernel, tiles, grps), out_shape=(jax.Sha...]
    mul x0 -> x1, other arithmetic: none -> 1.38 us  [body(): return (filtered, select.astype(jnp.float32) * surface)]
    unnamed x4 -> x3, local copies, waits for them, and re-layouts: 3.76 us -> 3.14 us
where the time goes in v2:
time: 120 us; the launch traced here: 118 us
  Pallas kernels  113 us (94%)
  local copies, waits for them, and re-layouts  3.14 us (3%)
  other arithmetic  1.38 us (1%)
    pallas_call x1, Pallas kernels, body(): pl.pallas_call(functools.partial(kernel, tiles, grps), out_shape=(jax.Sha...  113 us
    unnamed x3, local copies, waits for them, and re-layouts  3.14 us

profile of v2, /device:TPU:0, one launch (start us, length us, event | category | flops | bytes accessed | tf_op | source)
XLA Modules:
  0.0 118.3 jit_solution(1177260525548387673)
XLA Ops:
  0.6 0.0 copy-start
  0.6 113.1 %shard_map.86 = (f32[8,32,2048]{2,1,0:T(8,128)}, f32[32,256]{1,0:T(8,128)}) custom-call(f32[8,32,2048]{2,1,0:T(8,128)} %state_ref.1, f32[8,32,2048]{2,1,0:T(8,128)} %misfit_ref.1, f32[8,32,2048]{2,1,0:T(8,128)} %east_ref.1, f32[8,32,2048]{2,1,0:T(8,128)} %north_ref.1, s32[8,32,2048]{2,1,0:T(8,128)} %land_ref.1, f32[64,64]{1,0:T(8,128)} %matrix_ref.1), custom_call_target="tpu_custom_call" | custom-call | tf_op jit(solution)/shard_map/pallas_call | solution.py:356
  113.8 0.0 copy-done
  113.8 1.4 %convert_multiply_fusion = f32[32,256]{1,0:T(8,128)} fusion(f32[32,256]{1,0:T(8,128)} %get-tuple-element.5, s32[32,256]{1,0:T(8,128)S(1)} %copy-done), kind=kLoop, calls=%fused_computation | loop fusion | flops 16384 | bytes 98304 | tf_op jit(solution)/shard_map/mul | solution.py:389
  115.2 3.1 %copy.10 = f32[8,32,2048]{2,1,0:T(8,128)} copy(f32[8,32,2048]{2,1,0:T(8,128)} %get-tuple-element.8) | data formatting | bytes 4194304
Async XLA Ops:
  0.6 113.2 %copy-start = (s32[32,256]{1,0:T(8,128)S(1)}, s32[32,256]{1,0:T(8,128)}, u32[]{:S(2)}) copy-start(s32[32,256]{1,0:T(8,128)} %param.12) | copy-start | bytes 98308

commit v3 on v1

--- a/solution.py
+++ b/solution.py
@@ -22,7 +22,6 @@
     east_ref,
     north_ref,
     land_ref,
-    select_ref,
     matrix_ref,
     out_ref,
     surface_ref,
@@ -262,16 +261,16 @@
     advance(s1, s2, False, near, early, 1, chunks - 2)
     forward(near, early, 1, chunks - 2)
 
+    arrive(row_mid)
+    for r in (0, chunks - 1):
+        advance(s1, s2, False, near, early, r, 1)
+        forward(near, early, r, 1)
+
     arrive(level0)
     advance(s0, s1, True, 0, 1, 0, chunks)
     advance(s0, s1, True, levels - 1, 1, 0, chunks)
     start(level1)
     start(row_ends)
-
-    arrive(row_mid)
-    for r in (0, chunks - 1):
-        advance(s1, s2, False, near, early, r, 1)
-        forward(near, early, r, 1)
     advance(s1, s2, False, 1, near - 1, 0, chunks)
     advance(s1, s2, False, levels - near, near - 1, 0, chunks)
 
@@ -330,9 +329,7 @@
         pltpu.make_async_copy(
             smooth.at[pl.ds(tile * levels, levels), span, :], home, ret_recv
         ).start()
-        surface_ref[r * SUB : (r + 1) * SUB, :] = (
-            select_ref[r * SUB : (r + 1) * SUB, :].astype(jnp.float32) * result[0:SUB]
-        )
+        surface_ref[r * SUB : (r + 1) * SUB, :] = result[0:SUB]
 
     for copies in (level0, row0, level1, row_mid, row_ends):
         leave(copies)
@@ -344,6 +341,7 @@
 
 
 def body(tiles, grps, *args):
+    args, select = args[:5] + args[6:], args[5]
     levels, rows, columns = args[0].shape
     part = columns // tiles
     total = tiles * levels
@@ -351,13 +349,13 @@
     block = (levels, rows, columns)
     anywhere = pl.BlockSpec(memory_space=pl.ANY)
     vmem = pl.BlockSpec(memory_space=pltpu.VMEM)
-    return pl.pallas_call(
+    filtered, surface = pl.pallas_call(
         functools.partial(kernel, tiles, grps),
         out_shape=(
             jax.ShapeDtypeStruct(block, jnp.float32),
             jax.ShapeDtypeStruct((rows, part), jnp.float32),
         ),
-        in_specs=[anywhere] * 5 + [vmem] * 2,
+        in_specs=[anywhere] * 5 + [vmem],
         out_specs=(anywhere, vmem),
         scratch_shapes=[
             pltpu.VMEM(padded, jnp.float32),
@@ -384,6 +382,7 @@
             collective_id=0, has_side_effects=True, vmem_limit_bytes=56 * 1024 * 1024
         ),
     )(*args)
+    return filtered, select.astype(jnp.float32) * surface
 
 
 def solution(mesh):

time: 114 us -> 117 us (1.026)
  other arithmetic: 0 us -> 1.38 us
    mul x0 -> x1, other arithmetic: none -> 1.38 us  [body(): return (filtered, select.astype(jnp.float32) * surface)]
    unnamed x4 -> x3, local copies, waits for them, and re-layouts: 3.76 us -> 3.14 us
where the time goes in v3:
time: 117 us; the launch traced here: 115 us
  Pallas kernels  109 us (93%)
  local copies, waits for them, and re-layouts  3.14 us (3%)
  other arithmetic  1.38 us (1%)
    pallas_call x1, Pallas kernels, body(): pl.pallas_call(functools.partial(kernel, tiles, grps), out_shape=(jax.Sha...  109 us
    unnamed x3, local copies, waits for them, and re-layouts  3.14 us

profile of v3, /device:TPU:0, one launch (start us, length us, event | category | flops | bytes accessed | tf_op | source)
XLA Modules:
  0.0 114.6 jit_solution(10251188495573902518)
XLA Ops:
  0.6 0.0 copy-start
  0.6 109.4 %shard_map.86 = (f32[8,32,2048]{2,1,0:T(8,128)}, f32[32,256]{1,0:T(8,128)}) custom-call(f32[8,32,2048]{2,1,0:T(8,128)} %state_ref.1, f32[8,32,2048]{2,1,0:T(8,128)} %misfit_ref.1, f32[8,32,2048]{2,1,0:T(8,128)} %east_ref.1, f32[8,32,2048]{2,1,0:T(8,128)} %north_ref.1, s32[8,32,2048]{2,1,0:T(8,128)} %land_ref.1, f32[64,64]{1,0:T(8,128)} %matrix_ref.1), custom_call_target="tpu_custom_call" | custom-call | tf_op jit(solution)/shard_map/pallas_call | solution.py:352
  110.1 0.0 copy-done
  110.1 1.4 %convert_multiply_fusion = f32[32,256]{1,0:T(8,128)} fusion(f32[32,256]{1,0:T(8,128)} %get-tuple-element.5, s32[32,256]{1,0:T(8,128)S(1)} %copy-done), kind=kLoop, calls=%fused_computation | loop fusion | flops 16384 | bytes 98304 | tf_op jit(solution)/shard_map/mul | solution.py:385
  111.5 3.1 %copy.10 = f32[8,32,2048]{2,1,0:T(8,128)} copy(f32[8,32,2048]{2,1,0:T(8,128)} %get-tuple-element.8) | data formatting | bytes 4194304
Async XLA Ops:
  0.6 109.5 %copy-start = (s32[32,256]{1,0:T(8,128)S(1)}, s32[32,256]{1,0:T(8,128)}, u32[]{:S(2)}) copy-start(s32[32,256]{1,0:T(8,128)} %param.12) | copy-start | bytes 98308

commit v4 on v3

--- a/solution.py
+++ b/solution.py
@@ -249,28 +249,33 @@
     start(level0)
     for load in loads:
         load.wait()
-    arrive(row0)
-
-    advance(s0, s1, True, 1, levels - 2, 0, chunks)
+
     level1 = level_copies(s1, 1)
     row_mid = row_copies(s1, 1, 1, 1, levels - 2) if levels > 2 else []
     row_ends = row_copies(s1, 1, 2, 0, 1) + row_copies(s1, 1, 3, levels - 1, 1)
-    start(row_mid)
-
     early = levels - 2 * near
-    advance(s1, s2, False, near, early, 1, chunks - 2)
-    forward(near, early, 1, chunks - 2)
-
-    arrive(row_mid)
-    for r in (0, chunks - 1):
+    middle = chunks - 2
+    advance(s0, s1, True, 1, levels - 2, 1, middle)
+    arrive(row0)
+    advance(s0, s1, True, 1, levels - 2, 0, 1)
+    for r in range(1, middle):
         advance(s1, s2, False, near, early, r, 1)
         forward(near, early, r, 1)
+    advance(s0, s1, True, 1, levels - 2, chunks - 1, 1)
+    start(row_mid)
+    advance(s1, s2, False, near, early, middle, 1)
+    forward(near, early, middle, 1)
 
     arrive(level0)
     advance(s0, s1, True, 0, 1, 0, chunks)
     advance(s0, s1, True, levels - 1, 1, 0, chunks)
     start(level1)
     start(row_ends)
+
+    arrive(row_mid)
+    for r in (0, chunks - 1):
+        advance(s1, s2, False, near, early, r, 1)
+        forward(near, early, r, 1)
     advance(s1, s2, False, 1, near - 1, 0, chunks)
     advance(s1, s2, False, levels - near, near - 1, 0, chunks)
 

time: 117 us -> 115 us (0.983); the launches traced: 115 us -> 114 us
  no operation moved by 1% of the time
where the time goes in v4:
time: 115 us; the launch traced here: 114 us
  Pallas kernels  109 us (95%)
  local copies, waits for them, and re-layouts  3.14 us (3%)
  other arithmetic  1.38 us (1%)
    pallas_call x1, Pallas kernels, body(): pl.pallas_call(functools.partial(kernel, tiles, grps), out_shape=(jax.Sha...  109 us
    unnamed x3, local copies, waits for them, and re-layouts  3.14 us

profile of v4, /device:TPU:0, one launch (start us, length us, event | category | flops | bytes accessed | tf_op | source)
XLA Modules:
  0.0 114.2 jit_solution(14745003173291482266)
XLA Ops:
  0.6 0.0 copy-start
  0.6 109.0 %shard_map.86 = (f32[8,32,2048]{2,1,0:T(8,128)}, f32[32,256]{1,0:T(8,128)}) custom-call(f32[8,32,2048]{2,1,0:T(8,128)} %state_ref.1, f32[8,32,2048]{2,1,0:T(8,128)} %misfit_ref.1, f32[8,32,2048]{2,1,0:T(8,128)} %east_ref.1, f32[8,32,2048]{2,1,0:T(8,128)} %north_ref.1, s32[8,32,2048]{2,1,0:T(8,128)} %land_ref.1, f32[64,64]{1,0:T(8,128)} %matrix_ref.1), custom_call_target="tpu_custom_call" | custom-call | tf_op jit(solution)/shard_map/pallas_call | solution.py:357
  109.6 0.0 copy-done
  109.6 1.4 %convert_multiply_fusion = f32[32,256]{1,0:T(8,128)} fusion(f32[32,256]{1,0:T(8,128)} %get-tuple-element.5, s32[32,256]{1,0:T(8,128)S(1)} %copy-done), kind=kLoop, calls=%fused_computation | loop fusion | flops 16384 | bytes 98304 | tf_op jit(solution)/shard_map/mul | solution.py:390
  111.0 3.1 %copy.10 = f32[8,32,2048]{2,1,0:T(8,128)} copy(f32[8,32,2048]{2,1,0:T(8,128)} %get-tuple-element.8) | data formatting | bytes 4194304
Async XLA Ops:
  0.6 109.0 %copy-start = (s32[32,256]{1,0:T(8,128)S(1)}, s32[32,256]{1,0:T(8,128)}, u32[]{:S(2)}) copy-start(s32[32,256]{1,0:T(8,128)} %param.12) | copy-start | bytes 98308
